TPU v7x, 512 devices: a whole 4x4x16 slice. The times are simulated.
512 devices in a mesh: seq: 64 (over z, y), head: 8 (over x, core).
Axes of the slice: x: 4, y: 4, z: 16, core: 2. Of those that a mesh axis runs over, the one named last changes fastest.
Arguments:
- inner_acts: bfloat16 [16384, 8192], P('seq', 'head'), may hold values from -0.4375 to 0.4375
- out_grad: bfloat16 [16384, 8192], P('seq', 'head'), may hold values from -0.4375 to 0.4375
- write_proj: bfloat16 [16384, 128], P('seq'), may hold values from -3 to 3
- read_proj: bfloat16 [16384, 128], P('seq'), may hold values from -3 to 3
- log_decay: float32 [16384, 64], P('seq', 'head'), may hold values from -2.5 to 0, as said below
- w_in: bfloat16 [4096, 8192], P('seq', 'head'), may hold values from -0.1875 to 0.1875
Outputs:
- input_grad: bfloat16 [16384, 4096], P('seq', 'head')
- act_grad: bfloat16 [16384, 8192], P('seq', 'head')
- write_grad: float32 [16384, 128], P('seq')
- read_grad: float32 [16384, 128], P('seq')
Inputs may be any that keep to these rules, and one draw needn't show every extreme that they name: `log_decay`: natural log of a decay factor of each head at each token; every entry is negative.
All inputs are finite; a program needn't handle non-finite values.
Results may differ from a plain program's by a relative error of at most 0.019.
Values may be sent and summed in bfloat16 or wider, within the bound.
A program may use at most 192 MiB of HBM per device.

v0:
```python
import jax
import jax.numpy as jnp
from jax import lax
from jax.sharding import PartitionSpec as P

SPAN = 256


exact_mode = lax.Precision.HIGHEST


def carried_in(shard, axis, combine, identity):
    devices, position = (lax.axis_size(axis), lax.axis_index(axis))
    everything = jax.tree.map(
        lambda part, kind: lax.all_gather(part.astype(kind), axis),
        shard,
        (jnp.bfloat16, jnp.bfloat16),
    )
    start = jax.tree.map(
        lambda part, zero: jnp.broadcast_to(jnp.asarray(zero, part.dtype), part.shape),
        shard,
        identity,
    )

    def step(k, before):
        reached = k < position
        new = combine(
            before, jax.tree.map(lambda part, own: part[k].astype(own.dtype), everything, shard)
        )
        return jax.tree.map(lambda a, b: jnp.where(reached, a, b), new, before)

    return lax.fori_loop(0, devices, step, start)


def carried_in_2(part, axis, combine, identity):
    count = lax.axis_size(axis)
    place = lax.axis_index(axis)
    ahead = count - 1 - place
    gathered = jax.tree.map(lambda a: lax.all_gather(a, axis), part)
    state = jax.tree.map(lambda a, e: jnp.zeros_like(a) + jnp.asarray(e, a.dtype), part, identity)

    def one(step, state):
        source = count - 1 - step
        return combine(
            state, jax.tree.map(lambda a: lax.dynamic_index_in_dim(a, source, 0, False), gathered)
        )

    return lax.fori_loop(0, ahead, one, state)


def decay_blocks(cumulative):
    count = cumulative.shape[1]
    by_head = jnp.swapaxes(cumulative, 1, 2)
    spread_log = by_head[:, :, :, None] - by_head[:, :, None, :]
    below_diag = jnp.arange(count)[:, None] >= jnp.arange(count)[None, :]
    return jnp.exp(jnp.where(below_diag, spread_log, -jnp.inf))


def combine(earlier, later):
    return (earlier[0] + later[0], jnp.exp(later[0])[:, None, None] * earlier[1] + later[1])


def local(inner_acts, out_grad, write_proj, read_proj, log_decay, w_in):
    tok_rows = inner_acts.shape[0]
    head_count = log_decay.shape[1]
    head_dim = inner_acts.shape[1] // head_count
    state_dim = write_proj.shape[1]
    blocks = tok_rows // SPAN
    act_narrow = inner_acts.reshape(blocks, SPAN, head_count, head_dim)
    grad_narrow = out_grad.reshape(blocks, SPAN, head_count, head_dim)
    act_blocks = act_narrow.astype(jnp.float32)
    grad_blocks = grad_narrow.astype(jnp.float32)
    write_blocks = write_proj.astype(jnp.float32).reshape(blocks, SPAN, state_dim)
    read_blocks = read_proj.astype(jnp.float32).reshape(blocks, SPAN, state_dim)
    cumulative = jnp.cumsum(log_decay.reshape(blocks, SPAN, head_count), axis=1)
    totals = cumulative[:, -1, :]
    tail_decay = jnp.exp(totals[:, None, :] - cumulative)
    head_decay = jnp.exp(cumulative)
    decays = decay_blocks(cumulative)
    weighted = decays * jnp.einsum(
        "kahp,kbhp->khab", grad_narrow, act_narrow, preferred_element_type=jnp.float32
    )
    read_local = jnp.einsum("khab,kbn->kan", weighted, write_blocks, precision=exact_mode)
    write_local = jnp.einsum("khab,kan->kbn", weighted, read_blocks, precision=exact_mode)
    scores = jnp.einsum(
        "kan,kbn->kab",
        read_proj.reshape(blocks, SPAN, state_dim),
        write_proj.reshape(blocks, SPAN, state_dim),
        preferred_element_type=jnp.float32,
    )
    act_local = jnp.einsum(
        "khab,kahp->kbhp", decays * scores[:, None], grad_blocks, precision=exact_mode
    )
    block_ends = jnp.einsum(
        "kbhp,kbn->khpn", act_blocks * tail_decay[..., None], write_blocks, precision=exact_mode
    )
    fronts = jnp.einsum(
        "kahp,kan->khpn", grad_blocks * head_decay[..., None], read_blocks, precision=exact_mode
    )
    zero_log = jnp.zeros((head_count,), jnp.float32)
    zero_state = jnp.zeros((head_count, head_dim, state_dim), jnp.float32)
    prefix_logs = []
    prefix_states = []
    running = (zero_log, zero_state)
    index = 0
    prefix_logs.append(running[0])
    prefix_states.append(running[1])
    running = combine(running, (totals[index], block_ends[index]))
    end_log, end_state = running
    suffix_logs = [zero_log] * blocks
    suffix_grads = [zero_state] * blocks
    running = (zero_log, zero_state)
    for index in reversed(range(blocks)):
        suffix_logs[index] = running[0]
        suffix_grads[index] = running[1]
        running = combine(running, (totals[index], fronts[index]))
    front_log, front_state = running
    state_in = carried_in((end_log, end_state), "seq", combine, (zero_log, zero_state))[1]
    grad_in = carried_in_2((front_log, front_state), "seq", combine, (zero_log, zero_state))[1]
    current = state_in
    index = 0
    states_list = [current]
    grads_list = [zero_state] * blocks
    current = grad_in
    for index in reversed(range(blocks)):
        grads_list[index] = current
        current = jnp.exp(totals[index])[:, None, None] * current + fronts[index]
    state_stack = jnp.stack(states_list)
    grad_stack = jnp.stack(grads_list)
    read_carry = jnp.einsum(
        "kahp,khpn->kan", grad_blocks * head_decay[..., None], state_stack, precision=exact_mode
    )
    write_carry = jnp.einsum(
        "kbhp,khpn->kbn", act_blocks * tail_decay[..., None], grad_stack, precision=exact_mode
    )
    act_carry = (
        jnp.einsum("khpn,kbn->kbhp", grad_stack, write_blocks, precision=exact_mode)
        * tail_decay[..., None]
    )
    act_grad = (act_local + act_carry).astype(jnp.bfloat16).reshape(tok_rows, head_count * head_dim)
    write_part = (write_local + write_carry).reshape(tok_rows, state_dim)
    read_part = (read_local + read_carry).reshape(tok_rows, state_dim)
    write_grad, read_grad = (
        lax.psum(write_part.astype(jnp.bfloat16), "head").astype(jnp.float32),
        lax.psum(read_part.astype(jnp.bfloat16), "head").astype(jnp.float32),
    )
    group_term = lax.dot_general(
        act_grad,
        lax.all_gather(w_in, "seq", axis=0, tiled=True),
        (((1,), (1,)), ((), ())),
        preferred_element_type=jnp.float32,
    )
    input_grad = lax.psum_scatter(
        group_term.astype(jnp.bfloat16).astype(jnp.float32).astype(jnp.bfloat16),
        "head",
        scatter_dimension=1,
        tiled=True,
    )
    return (input_grad, act_grad, write_grad, read_grad)


def solution(mesh):
    return jax.shard_map(
        local,
        mesh=mesh,
        in_specs=(
            P("seq", "head"),
            P("seq", "head"),
            P("seq", None),
            P("seq", None),
            P("seq", "head"),
            P("seq", "head"),
        ),
        out_specs=(P("seq", "head"), P("seq", "head"), P("seq", None), P("seq", None)),
        check_vma=False,
    )
```

profile of v0, /device:TPU:1, one launch (start us, length us, event | category | flops | bytes accessed | tf_op | source)
XLA Modules:
  0.0 783.9 jit_solution(3327351343411042735)
XLA Ops:
  7.2 1.3 reduce-window.6
  11.4 1.3 fusion.14
  13.1 1.8 convolution_add_fusion.1
  17.9 74.9 %all-gather = f32[64,1,8]{2,1,0:T(1,128)} all-gather(f32[1,1,8]{2,1,0:T(1,128)S(1)} %copy-done.7), channel_id=2, replica_groups=mesh['seq'=64,'head'=8] {'seq'}, dimensions={0}, use_global_device_ids=true | all-gather | bytes 2080 | tf_op jit(solution)/shard_map/all_gather | solution.py:39
  94.1 63.8 %all-gather.3 = bf16[64,1,8]{2,1,0:T(2,128)(2,1)S(1)} all-gather(bf16[1,1,8]{2,1,0:T(2,128)(2,1)} %slice.19), channel_id=5, replica_groups=mesh['seq'=64,'head'=8] {'seq'}, dimensions={0}, use_global_device_ids=true | all-gather | bytes 1040 | tf_op jit(solution)/shard_map/all_gather | solution.py:15
  158.5 1.7 multiply_reduce_fusion
  160.3 51.7 %all-gather.12.cloned.1.call-done = bf16[512,128,128]{2,1,0:T(8,128)(2,1)} async-done(((bf16[8,128,128]{2,1,0:T(8,128)(2,1)}), bf16[512,128,128]{2,1,0:T(8,128)(2,1)}) %all-gather.12.cloned.1.call-update) | async-done | bytes 16777232 | tf_op jit(solution)/shard_map/all_gather | solution.py:15
  212.0 115.6 %while.29 = (s32[]{:T(128)}, f32[8,128,128]{2,1,0:T(8,128)S(1)}, s32[]{:T(128)}, bf16[64,8]{1,0:T(8,128)(2,1)}, bf16[64,8,128,128]{3,2,1,0:T(8,128)(2,1)}, /*index=5*/s32[]{:T(128)}, s32[]{:T(128)}) while((s32[]{:T(128)}, f32[8,128,128]{2,1,0:T(8,128)S(1)}, s32[]{:T(128)}, bf16[64,8]{1,0:T(8,128)(2,1)}, ...), condition=%wide.region_8.9_spmd.clone, body=%wide.region_7.8_spmd.clone.sunk | while | flops 655372 | bytes 1310905 | solution.py:32
  329.6 176.4 %all-gather.10.cloned.1.call-done = f32[512,128,128]{2,1,0:T(8,128)} async-done(((f32[8,128,128]{2,1,0:T(8,128)}), f32[512,128,128]{2,1,0:T(8,128)}) %all-gather.10.cloned.1.call-update) | async-done | bytes 33554448 | tf_op jit(solution)/shard_map/all_gather | solution.py:39
  506.1 120.2 %while.28 = (s32[]{:T(128)}, f32[8,128,128]{2,1,0:T(8,128)S(1)}, s32[]{:T(128)}, f32[64,8]{1,0:T(8,128)}, f32[64,8,128,128]{3,2,1,0:T(8,128)}, /*index=5*/s32[]{:T(128)}, s32[]{:T(128)}, s32[]{:T(128)}, s32[]{:T(128)}) while((s32[]{:T(128)}, f32[8,128,128]{2,1,0:T(8,128)S(1)}, s32[]{:T(128)}, f32[64,8]{1,0:T(8,128)}, ...), condition=%wide.region_3.4_spmd, body=%wide.region_2.3_spmd.sunk | while | flops 262150 | bytes 1573107 | solution.py:48
  522.0 1.2 bitcast_add_fusion.5
  527.8 1.2 bitcast_add_fusion.5
  531.6 1.2 bitcast_add_fusion.5
  537.3 1.2 bitcast_add_fusion.5
  546.8 1.2 bitcast_add_fusion.5
  548.8 1.2 bitcast_add_fusion.5
  558.3 1.2 bitcast_add_fusion.5
  565.9 1.2 bitcast_add_fusion.5
  592.5 1.2 bitcast_add_fusion.5
  602.1 1.2 bitcast_add_fusion.5
  607.8 1.2 bitcast_add_fusion.5
  613.6 1.2 bitcast_add_fusion.5
  619.3 1.2 bitcast_add_fusion.5
  621.3 1.2 bitcast_add_fusion.5
  626.9 1.8 convolution_bitcast_fusion.2
  629.8 2.4 fusion.11
  632.5 22.6 %all-gather.8.cloned.1.call-done = bf16[4096,1024]{1,0:T(8,128)(2,1)} async-done(((bf16[64,1024]{1,0:T(8,128)(2,1)}), bf16[4096,1024]{1,0:T(8,128)(2,1)}) %all-gather.8.cloned.1.call-update) | async-done | bytes 8388624 | tf_op jit(solution)/shard_map/all_gather | solution.py:149
  655.1 7.1 convolution_convert_fusion
  663.2 70.7 %all-reduce.3.cloned.1.call-done = (bf16[256,128]{1,0:T(8,128)(2,1)}, bf16[256,128]{1,0:T(8,128)(2,1)}) async-done(((bf16[256,128]{1,0:T(8,128)(2,1)}, bf16[256,128]{1,0:T(8,128)(2,1)}), (bf16[256,128]{1,0:T(8,128)(2,1)}, bf16[256,128]{1,0:T(8,128)(2,1)})) %all-reduce.3.cloned.1.call-update) | async-done | bytes 131088 | tf_op jit(solution)/shard_map/psum | solution.py:144
  733.9 1.5 convert_element_type.84
  735.4 1.5 convert_element_type.89
  736.9 40.5 %reduce-scatter.2.cloned.1.call-done = bf16[256,512]{1,0:T(8,128)(2,1)} async-done(((bf16[256,4096]{1,0:T(8,128)(2,1)}), bf16[256,512]{1,0:T(8,128)(2,1)}) %reduce-scatter.2.cloned.1.call-update) | async-done | bytes 262160 | tf_op jit(solution)/shard_map/reduce_scatter | solution.py:153
  (294 shorter events, 229.0 us)
Async XLA Ops:
  7.2 3.9 copy-start
  7.2 3.3 copy-start.3
  7.2 204.8 %all-gather.12.cloned.1.call-start = ((), (), s32[]{:S(2)}) async-start(), calls=%async_computation.4 | async-start | bytes 17039360 | tf_op jit(solution)/shard_map/all_gather | solution.py:15
  8.8 1.8 copy-start.4
  10.7 0.7 copy-start.6
  10.7 2.4 copy-start.1
  10.7 2.4 copy-start.2
  12.7 493.3 %all-gather.10.cloned.1.call-start = ((), (), s32[]{:S(2)}) async-start(), calls=%async_computation.3 | async-start | bytes 34078720 | tf_op jit(solution)/shard_map/all_gather | solution.py:39
  13.1 4.8 copy-start.7
  15.0 640.1 %all-gather.8.cloned.1.call-start = ((), (), s32[]{:S(2)}) async-start(), calls=%async_computation.1 | async-start | bytes 8519680 | tf_op jit(solution)/shard_map/all_gather | solution.py:149
  15.7 718.1 %all-reduce.3.cloned.1.call-start = ((), (), s32[]{:S(2)}) async-start(), calls=%async_computation.5 | async-start | bytes 262144 | tf_op jit(solution)/shard_map/psum | solution.py:144
  626.3 3.4 copy-start.5
  632.2 145.1 %reduce-scatter.2.cloned.1.call-start = ((), (), s32[]{:S(2)}) async-start(), calls=%async_computation.2 | async-start | bytes 2359296 | tf_op jit(solution)/shard_map/reduce_scatter | solution.py:153
Sparse Core Ops, SparseCore 0:
  12.8 199.0 all-gather.11
  215.5 290.5 all-gather.9
  509.0 146.0 all-gather.7
  657.9 75.9 all-reduce.2
  737.4 39.9 reduce-scatter.1
where the time goes:
time: 794 us; the launch traced here: 784 us
  waiting for transfers between devices  363 us (46%)
  other arithmetic  196 us (25%)
  blocking collectives  139 us (18%)
  local copies, waits for them, and re-layouts  48.7 us (6%)
  matrix products  20.7 us (3%)
  between operations  14 us (2%)
    all_gather x1, waiting for transfers between devices, carried_in_2(): gathered = jax.tree.map(lambda a: lax.all_gather(a, axis), part)  176 us
    add x63, other arithmetic, combine(): jnp.exp(later[0])[:, None, None] * earlier[1] + later[1]  75 us
    all_gather x1, blocking collectives, carried_in_2(): gathered = jax.tree.map(lambda a: lax.all_gather(a, axis), part)  74.9 us
    psum x1, waiting for transfers between devices, local(): lax.psum(write_part.astype(jnp.bfloat16), 'head').astype(jnp.float32)  70.7 us
    select_n x64, other arithmetic, step(): return jax.tree.map(lambda a, b: jnp.where(reached, a, b), new, before)  70.1 us
    all_gather x1, blocking collectives, carried_in(): lax.all_gather(part.astype(kind), axis)  63.8 us
    all_gather x1, waiting for transfers between devices, carried_in(): lax.all_gather(part.astype(kind), axis)  51.7 us
    exp x64, other arithmetic, combine(): jnp.exp(later[0])[:, None, None] * earlier[1] + later[1]  44.4 us
  transfers between devices with their start and end apart: 5, of which 5 were waited for; matrix products, arithmetic and copies ran while one was open for 33% of the time, Pallas kernels for 0%

commit v1 on v0

v1 whole, which is shorter than its diff:
```python
import functools

import jax
import jax.numpy as jnp
from jax import lax
from jax.experimental import pallas as pl
from jax.experimental.pallas import tpu as pltpu
from jax.sharding import PartitionSpec as P

MESH = pl.DeviceIdType.MESH
F32, BF16 = jnp.float32, jnp.bfloat16
Y = 4
T = 256
H = 8
K = 128
ROWS = 64

NN = (((1,), (0,)), ((), ()))
NT = (((1,), (1,)), ((), ()))
TN = (((0,), (0,)), ((), ()))


def dot(a, b, dims=NN):
    return lax.dot_general(a, b, dims, preferred_element_type=F32)


def remote(src, dst, send, recv, device):
    return pltpu.make_async_remote_copy(
        src, dst, send, recv, device_id=device, device_id_type=MESH
    )


def kernel(
    Z, X,
    x_ref, dy_ref, b_ref, c_ref, log_ref, w_ref,
    out_ref, act_ref, wg_ref, rg_ref,
    cs_ref, xs_ref, dys_ref, actl_ref, wt_ref,
    csall, ball, actl_all, tb_ref, atot,
    wz, up_s, up_r, dz_s, dz_r, zs, zr, cz, zin,
    g_s, g_r, st_s, st_r, act_all,
    co_s, co_r, keep, x_s, x_r, y_s, y_r,
    p_s, p_r, px, pf, pf_r, part_ref,
    y_ss, y_rs, w_ss, w_rs, z_ss, z_rs, c_ss, c_rs, x_ss, x_rs,
):
    seq, head = lax.axis_index("seq"), lax.axis_index("head")
    z, y = seq // Y, lax.rem(seq, Y)
    cx, core = head // 2, lax.rem(head, 2)

    def at_z(d):
        return (lax.rem(z + d + Z, Z) * Y + y, head)

    def y_of(d):
        return lax.rem(y + d + Y, Y)

    def at_y(d):
        return (z * Y + y_of(d), head)

    def x_of(d):
        return lax.rem(cx + d + X, X)

    def at_x(d):
        return (seq, x_of(d) * 2 + core)

    other = (seq, cx * 2 + 1 - core)

    barrier = pltpu.get_barrier_semaphore()
    partners = (
        [at_y(d) for d in range(1, Y)]
        + [at_x(d) for d in range(1, X)]
        + [other]
    )
    for device in partners:
        pl.semaphore_signal(barrier, inc=1, device_id=device, device_id_type=MESH)

    def greet(d, carry):
        pl.semaphore_signal(barrier, inc=1, device_id=at_z(d), device_id_type=MESH)
        return carry

    lax.fori_loop(1, Z, greet, 0)

    rows = lax.broadcasted_iota(jnp.int32, (T, T), 0)
    lanes = lax.broadcasted_iota(jnp.int32, (T, T), 1)
    lower = jnp.where(rows >= lanes, 1.0, 0.0).astype(F32)
    logs = jnp.concatenate([log_ref[...], jnp.zeros((T, K - H), F32)], axis=1)
    cs = lax.dot_general(
        lower, logs, NN, precision=lax.Precision.HIGHEST, preferred_element_type=F32
    )
    cs_ref[...] = cs
    cs_rows = cs.T[0:H]
    csall[y] = cs_rows
    ball[y] = b_ref[...]
    wz[z] = w_ref[...]
    tail = jnp.exp(cs[T - 1 : T] - cs)
    front = jnp.exp(cs)
    for h in range(H):
        cut = slice(h * K, (h + 1) * K)
        xs_ref[:, cut] = (x_ref[:, cut].astype(F32) * tail[:, h : h + 1]).astype(BF16)
        dys_ref[:, cut] = (dy_ref[:, cut].astype(F32) * front[:, h : h + 1]).astype(BF16)
    for i, (left, right) in enumerate(((b_ref, xs_ref), (c_ref, dys_ref))):
        total = dot(left[...], right[...], TN).astype(BF16)
        for h in range(H):
            up_s[h // 2, i, (h % 2) * K : (h % 2 + 1) * K] = total[:, h * K : (h + 1) * K]
    up_r[y] = up_s[y]

    pl.semaphore_wait(barrier, Y - 1 + X - 1 + 1 + Z - 1)

    half = Z // 2

    def w_copies(k):
        a, b = lax.rem(z - k + Z, Z), lax.rem(z + k, Z)
        if k < half - 1:
            fore, back = wz.at[a], wz.at[b]
        else:
            fore, back = wz.at[a, 0 : ROWS // 2], wz.at[b, ROWS // 2 : ROWS]
        return (
            remote(fore, fore, w_ss.at[0, k], w_rs.at[0, k], at_z(1)),
            remote(back, back, w_ss.at[1, k], w_rs.at[1, k], at_z(-1)),
        )

    def w_arrived(k):
        a, b = lax.rem(z - 1 - k + Z, Z), lax.rem(z + 1 + k, Z)
        if k < half - 1:
            fore, back = wz.at[a], wz.at[b]
        else:
            fore, back = wz.at[a, 0 : ROWS // 2], wz.at[b, ROWS // 2 : ROWS]
        remote(fore, fore, w_ss.at[0, k], w_rs.at[0, k], at_z(1)).wait_recv()
        remote(back, back, w_ss.at[1, k], w_rs.at[1, k], at_z(-1)).wait_recv()

    def w_step(k):
        if k > 0:
            w_arrived(k - 1)
        for copy in w_copies(k):
            copy.start()

    started = []

    def y_send(group, src_of, dst_of):
        for d in (2, 1, 3):
            copy = remote(
                src_of(y_of(d)), dst_of(y), y_ss.at[group, d], y_rs.at[group, d], at_y(d)
            )
            copy.start()
            started.append(copy)

    def y_wait(group, src_of, dst_of):
        for d in (1, 3, 2):
            remote(
                src_of(y_of(d)), dst_of(y_of(-d)), y_ss.at[group, d], y_rs.at[group, d], at_y(d)
            ).wait_recv()

    y_send(0, lambda t: csall.at[y], lambda s: csall.at[s])
    y_send(1, lambda t: up_s.at[t], lambda s: up_r.at[s])
    y_send(2, lambda t: ball.at[y], lambda s: ball.at[s])
    w_step(0)

    below = lanes >= rows
    scores = dot(b_ref[...], c_ref[...], NT)

    def heads(low, high):
        for h in range(low, high):
            cut = slice(h * K, (h + 1) * K)
            xh, dyh = x_ref[:, cut], dy_ref[:, cut]
            decay = jnp.exp(
                jnp.where(below, csall[y, h : h + 1, :] - cs_ref[:, h : h + 1], -jnp.inf)
            )
            weighted = decay * dot(xh, dyh, NT)
            wt_ref[...] = weighted if h == 0 else wt_ref[...] + weighted
            own = dot((decay * scores).astype(BF16), dyh)
            actl_ref[:, cut] = own
            actl_all[y, :, cut] = own.astype(BF16)

    heads(0, 4)
    y_wait(0, lambda t: csall.at[y], lambda s: csall.at[s])
    for t in range(Y):
        atot[t] = jnp.broadcast_to(csall[t][:, T - 1 : T], (H, K))

    def total_of(t, i):
        return atot[t, pl.ds(2 * y + i, 1), :]

    for i in range(2):
        plane = total_of(0, i) + total_of(1, i) + total_of(2, i) + total_of(3, i)
        dz_s[4 * i : 4 * i + 4] = jnp.broadcast_to(plane, (4, K))
    dz_r[z] = dz_s[...]

    def z_send(group, src_of, dst):
        def one(d, carry):
            t = lax.rem(z + d, Z)
            remote(
                src_of(t), dst.at[z], z_ss.at[group, d], z_rs.at[group, d], at_z(d)
            ).start()
            return carry

        lax.fori_loop(1, Z, one, 0)

    def z_wait(group, src_of, dst):
        def one(d, carry):
            remote(
                src_of(lax.rem(z + d, Z)), dst.at[lax.rem(z - d + Z, Z)],
                z_ss.at[group, d], z_rs.at[group, d], at_z(d),
            ).wait_recv()
            return carry

        lax.fori_loop(1, Z, one, 0)

    def z_sent(group, src_of, dst):
        def one(d, carry):
            remote(
                src_of(lax.rem(z + d, Z)), dst.at[z],
                z_ss.at[group, d], z_rs.at[group, d], at_z(d),
            ).wait_send()
            return carry

        lax.fori_loop(1, Z, one, 0)

    z_send(0, lambda t: dz_s, dz_r)
    w_step(1)
    heads(4, 8)
    w_step(2)

    y_wait(1, lambda t: up_s.at[t], lambda s: up_r.at[s])
    for i in range(2):
        cut = slice(i * K, (i + 1) * K)
        part = slice(i * (Z // 2), (i + 1) * (Z // 2))
        fore = up_r[0, 0, cut].astype(F32)
        back = up_r[Y - 1, 1, cut].astype(F32)
        for t in range(1, Y):
            fore = jnp.exp(total_of(t, i)) * fore + up_r[t, 0, cut].astype(F32)
            back = jnp.exp(total_of(Y - 1 - t, i)) * back + up_r[Y - 1 - t, 1, cut].astype(F32)
        zs[part, 0] = fore.astype(BF16).reshape(Z // 2, 2 * K // Z, K)
        zs[part, 1] = back.astype(BF16).reshape(Z // 2, 2 * K // Z, K)
    zr[z] = zs[z]
    z_send(1, lambda t: zs.at[t], zr)
    y_send(3, lambda t: actl_all.at[y], lambda s: actl_all.at[s])

    y_wait(2, lambda t: ball.at[y], lambda s: ball.at[s])

    def tails(t, carry):
        padded = jnp.concatenate([csall[t], jnp.zeros((K - H, T), F32)], axis=0)
        ct = padded.T
        et = jnp.exp(ct[T - 1 : T] - ct)
        bt = ball[t].astype(F32)
        for h in range(H):
            tb_ref[t, h] = (et[:, h : h + 1] * bt).astype(BF16)
        return carry

    lax.fori_loop(0, Y, tails, 0)
    wt = wt_ref[...]
    part_ref[0] = dot(wt.astype(BF16), c_ref[...])
    part_ref[1] = dot(wt.T.astype(BF16), b_ref[...])

    z_wait(0, lambda t: dz_s, dz_r)
    w_step(3)
    z_wait(1, lambda t: zs.at[t], zr)

    row = 4 * (z // (Z // 2))

    def sweep(k, carry):
        fore, back = carry
        j = Z - 1 - k
        cz[k, 0] = fore.astype(BF16)
        cz[j, 1] = back.astype(BF16)
        fore = jnp.exp(dz_r[k, pl.ds(row, 1), :]) * fore + zr[k, 0].astype(F32)
        back = jnp.exp(dz_r[j, pl.ds(row, 1), :]) * back + zr[j, 1].astype(F32)
        return fore, back

    zero = jnp.zeros((2 * K // Z, K), F32)
    lax.fori_loop(0, Z, sweep, (zero, zero))
    zin[z] = cz[z]
    z_send(2, lambda t: cz.at[t], zin)
    w_step(4)
    w_step(5)
    z_wait(2, lambda t: cz.at[t], zin)

    for i in range(2):
        cut = slice(i * K, (i + 1) * K)
        part = slice(i * (Z // 2), (i + 1) * (Z // 2))
        back = zin[part, 1].reshape(K, K).astype(F32)
        for t in reversed(range(Y)):
            g_s[t, cut] = back.astype(BF16)
            back = jnp.exp(total_of(t, i)) * back + up_r[t, 1, cut].astype(F32)
    g_r[y] = g_s[...]
    y_send(4, lambda t: g_s, lambda s: g_r.at[s])
    for i in range(2):
        cut = slice(i * K, (i + 1) * K)
        part = slice(i * (Z // 2), (i + 1) * (Z // 2))
        fore = zin[part, 0].reshape(K, K).astype(F32)
        for t in range(Y):
            st_s[t, cut] = fore.astype(BF16)
            fore = jnp.exp(total_of(t, i)) * fore + up_r[t, 0, cut].astype(F32)
    st_r[y] = st_s[y]
    y_send(5, lambda t: st_s.at[t], lambda s: st_r.at[s])
    for k in range(6, half):
        w_step(k)
    y_wait(3, lambda t: actl_all.at[y], lambda s: actl_all.at[s])
    w_arrived(half - 1)
    y_wait(4, lambda t: g_s, lambda s: g_r.at[s])
    y_wait(5, lambda t: st_s.at[t], lambda s: st_r.at[s])

    order = (2, 1, 3, 0)

    def core_copy(k):
        return remote(co_s.at[k], co_r.at[k], c_ss.at[k], c_rs.at[k], other)

    def stage_a(k):
        d = order[k]
        t = y_of(d)
        for h in range(H):
            cut = slice(h * K, (h + 1) * K)
            carried = dot(tb_ref[t, h], g_r[h // 2, t, (h % 2) * K : (h % 2 + 1) * K])
            if d == 0:
                own = (actl_ref[:, cut] + carried).astype(BF16)
                act_ref[:, cut] = own
            else:
                own = (actl_all[t, :, cut].astype(F32) + carried).astype(BF16)
            act_all[k, :, cut] = own
        act = act_all[k]
        per = Z // X
        for j in range(X):
            w = wz[per * j : per * (j + 1)].reshape(per * ROWS, H * K)
            both = dot(act, w, NT)
            low, high = both[:, 0:K], both[:, K : 2 * K]
            keep[k, j] = jnp.where(core == 0, low, high)
            co_s[k, j] = jnp.where(core == 0, high, low).astype(BF16)
        core_copy(k).start()

    def x_copies(k):
        return [
            remote(
                x_s.at[k, x_of(e)], x_r.at[k, e], x_ss.at[k, e], x_rs.at[k, e], at_x(e)
            )
            for e in range(1, X)
        ]

    def stage_b(k):
        core_copy(k).wait_recv()
        for j in range(X):
            total = keep[k, j] + co_r[k, j].astype(F32)
            keep[k, j] = total
            x_s[k, j] = total.astype(BF16)
        for copy in x_copies(k):
            copy.start()

    def y_copy(k):
        d = order[k]
        return remote(y_s.at[k], y_r.at[y], y_ss.at[6, d], y_rs.at[6, d], at_y(d))

    def stage_c(k):
        total = keep[k, cx]
        for e, copy in enumerate(x_copies(k), 1):
            copy.wait_recv()
            total = total + x_r[k, e].astype(F32)
        if order[k] == 0:
            y_r[y] = total.astype(BF16)
        else:
            y_s[k] = total.astype(BF16)
            y_copy(k).start()

    core_part = remote(p_s, p_r, c_ss.at[4], c_rs.at[4], other)
    core_total = remote(pf, pf_r, c_ss.at[5], c_rs.at[5], other)

    def parts_start():
        state = [st_r[h // 2, (h % 2) * K : (h % 2 + 1) * K] for h in range(H)]
        grad = [g_r[h // 2, y, (h % 2) * K : (h % 2 + 1) * K] for h in range(H)]
        write = part_ref[0] + dot(xs_ref[...], jnp.concatenate(grad, axis=1), NT)
        read = part_ref[1] + dot(dys_ref[...], jnp.concatenate(state, axis=1), NT)
        part_ref[0] = jnp.where(core == 0, write, read)
        p_s[...] = jnp.where(core == 0, read, write).astype(BF16)
        core_part.start()

    def part_copy(e):
        return remote(px.at[cx], px.at[cx], x_ss.at[4, e], x_rs.at[4, e], at_x(e))

    def parts_x():
        core_part.wait_recv()
        px[cx] = (part_ref[0] + p_r[...].astype(F32)).astype(BF16)
        for e in range(1, X):
            part_copy(e).start()

    def parts_core():
        for e in range(1, X):
            s = x_of(-e)
            remote(px.at[cx], px.at[s], x_ss.at[4, e], x_rs.at[4, e], at_x(e)).wait_recv()
        total = px[0].astype(F32)
        for j in range(1, X):
            total = total + px[j].astype(F32)
        pf[...] = total
        core_total.start()

    stage_a(0)
    parts_start()
    stage_a(1)
    stage_b(0)
    parts_x()
    stage_a(2)
    stage_b(1)
    stage_c(0)
    stage_a(3)
    stage_b(2)
    parts_core()
    stage_c(1)
    stage_b(3)
    stage_c(2)
    stage_c(3)
    core_total.wait_recv()
    wg_ref[...] = jnp.where(core == 0, pf[...], pf_r[...])
    rg_ref[...] = jnp.where(core == 0, pf_r[...], pf[...])
    for k in range(3):
        d = order[k]
        remote(
            y_s.at[k], y_r.at[y_of(-d)], y_ss.at[6, d], y_rs.at[6, d], at_y(d)
        ).wait_recv()
    for i in range(2):
        pieces = [y_r[t, :, i * ROWS : (i + 1) * ROWS] for t in range(Y)]
        out_ref[:, 2 * i * K : 2 * (i + 1) * K] = jnp.concatenate(pieces, axis=1)

    for copy in started:
        copy.wait_send()
    for k in range(half):
        for copy in w_copies(k):
            copy.wait_send()
    z_sent(0, lambda t: dz_s, dz_r)
    z_sent(1, lambda t: zs.at[t], zr)
    z_sent(2, lambda t: cz.at[t], zin)
    for k in range(4):
        core_copy(k).wait_send()
        for copy in x_copies(k):
            copy.wait_send()
        if order[k]:
            y_copy(k).wait_send()
    core_part.wait_send()
    core_total.wait_send()
    for e in range(1, X):
        part_copy(e).wait_send()


def solution(mesh):
    Z, X = mesh.shape["seq"] // Y, mesh.shape["head"] // 2
    piece = 2 * K // Z
    vmem, dma = pltpu.VMEM, pltpu.SemaphoreType.DMA

    def local(inner_acts, out_grad, write_proj, read_proj, log_decay, w_in):
        scratch = [
            vmem((T, K), F32),
            vmem((T, H * K), BF16),
            vmem((T, H * K), BF16),
            vmem((T, H * K), F32),
            vmem((T, T), F32),
            vmem((Y, H, T), F32),
            vmem((Y, T, K), BF16),
            vmem((Y, T, H * K), BF16),
            vmem((Y, H, T, K), BF16),
            vmem((Y, H, K), F32),
            vmem((Z, ROWS, H * K), BF16),
            vmem((Y, 2, 2 * K, K), BF16),
            vmem((Y, 2, 2 * K, K), BF16),
            vmem((8, K), F32),
            vmem((Z, 8, K), F32),
            vmem((Z, 2, piece, K), BF16),
            vmem((Z, 2, piece, K), BF16),
            vmem((Z, 2, piece, K), BF16),
            vmem((Z, 2, piece, K), BF16),
            vmem((Y, 2 * K, K), BF16),
            vmem((Y, Y, 2 * K, K), BF16),
            vmem((Y, 2 * K, K), BF16),
            vmem((Y, 2 * K, K), BF16),
            vmem((Y, T, H * K), BF16),
            vmem((Y, X, T, K), BF16),
            vmem((Y, X, T, K), BF16),
            vmem((Y, X, T, K), F32),
            vmem((Y, X, T, K), BF16),
            vmem((Y, X, T, K), BF16),
            vmem((Y, T, K), BF16),
            vmem((Y, T, K), BF16),
            vmem((T, K), BF16),
            vmem((T, K), BF16),
            vmem((X, T, K), BF16),
            vmem((T, K), F32),
            vmem((T, K), F32),
            vmem((2, T, K), F32),
            dma((7, Y)), dma((7, Y)),
            dma((2, Z // 2)), dma((2, Z // 2)),
            dma((3, Z)), dma((3, Z)),
            dma((6,)), dma((6,)),
            dma((5, X)), dma((5, X)),
        ]
        whole = pl.BlockSpec(memory_space=pltpu.VMEM)
        columns = w_in.shape[0] * mesh.shape["seq"] // mesh.shape["head"]
        return pl.pallas_call(
            functools.partial(kernel, Z, X),
            out_shape=(
                jax.ShapeDtypeStruct((T, columns), BF16),
                jax.ShapeDtypeStruct((T, H * K), BF16),
                jax.ShapeDtypeStruct((T, K), F32),
                jax.ShapeDtypeStruct((T, K), F32),
            ),
            in_specs=[whole] * 6,
            out_specs=(whole,) * 4,
            scratch_shapes=scratch,
            compiler_params=pltpu.CompilerParams(
                collective_id=0, has_side_effects=True, vmem_limit_bytes=56 * 2**20
            ),
        )(inner_acts, out_grad, write_proj, read_proj, log_decay, w_in)

    return jax.shard_map(
        local,
        mesh=mesh,
        in_specs=(
            P("seq", "head"),
            P("seq", "head"),
            P("seq", None),
            P("seq", None),
            P("seq", "head"),
            P("seq", "head"),
        ),
        out_specs=(P("seq", "head"), P("seq", "head"), P("seq", None), P("seq", None)),
        check_vma=False,
    )
```

time: 794 us -> 96.9 us (0.12); the launches traced: 784 us -> 96.6 us
  waiting for transfers between devices: 363 us -> 0 us
  other arithmetic: 196 us -> 0 us
  blocking collectives: 139 us -> 0 us
  Pallas kernels: 0 us -> 90.1 us
  local copies, waits for them, and re-layouts: 48.7 us -> 5.84 us
  matrix products: 20.7 us -> 0 us
  between operations: 14 us -> 0.65 us
    all_gather x3 -> x0, waiting for transfers between devices: 251 us -> none  [the longest x1 176 us: carried_in_2(): gathered = jax.tree.map(lambda a: lax.all_gather(a, axis), part)]
    all_gather x2 -> x0, blocking collectives: 139 us -> none  [the longest x1 74.9 us: carried_in_2(): gathered = jax.tree.map(lambda a: lax.all_gather(a, axis), part)]
    pallas_call x0 -> x1, Pallas kernels: none -> 90.1 us  [local(): pl.pallas_call(functools.partial(kernel, Z, X), out_shape=(jax.ShapeDtype...]
    add x63 -> x0, other arithmetic: 75 us -> none  [combine(): jnp.exp(later[0])[:, None, None] * earlier[1] + later[1]]
    psum x1 -> x0, waiting for transfers between devices: 70.7 us -> none  [local(): lax.psum(write_part.astype(jnp.bfloat16), 'head').astype(jnp.float32)]
    select_n x64 -> x0, other arithmetic: 70.1 us -> none  [step(): return jax.tree.map(lambda a, b: jnp.where(reached, a, b), new, before)]
    exp x64 -> x0, other arithmetic: 44.4 us -> none  [combine(): jnp.exp(later[0])[:, None, None] * earlier[1] + later[1]]
    exp x63 -> x0, local copies, waits for them, and re-layouts: 43.4 us -> none  [combine(): jnp.exp(later[0])[:, None, None] * earlier[1] + later[1]]
  transfers between devices with their start and end apart: 5 -> 0, of which waited for: 5 -> 0; matrix products, arithmetic and copies ran while one was open for 33% -> 0% of each run, Pallas kernels for 0% -> 0%
where the time goes in v1:
time: 96.9 us; the launch traced here: 96.6 us
  Pallas kernels  90.1 us (93%)
  local copies, waits for them, and re-layouts  5.84 us (6%)
    pallas_call x1, Pallas kernels, local(): pl.pallas_call(functools.partial(kernel, Z, X), out_shape=(jax.ShapeDtype...  90.1 us
    unnamed x11, local copies, waits for them, and re-layouts  5.84 us

profile of v1, /device:TPU:1, one launch (start us, length us, event | category | flops | bytes accessed | tf_op | source)
XLA Modules:
  0.0 96.6 jit_solution(3162760215804167987)
XLA Ops:
  0.6 1.5 %copy.10.log_ref = f32[256,8]{1,0:T(8,128)} copy(f32[256,8]{0,1:T(8,128)} %param.10) | data formatting | bytes 16384 | tf_op args[4]
  2.1 90.1 %shard_map.93 = (bf16[256,512]{1,0:T(8,128)(2,1)}, bf16[256,1024]{1,0:T(8,128)(2,1)}, f32[256,128]{1,0:T(8,128)}, f32[256,128]{1,0:T(8,128)}) custom-call(bf16[256,1024]{1,0:T(8,128)(2,1)} %x_ref.1, bf16[256,1024]{1,0:T(8,128)(2,1)} %dy_ref.1, bf16[256,128]{1,0:T(8,128)(2,1)} %b_ref.1, bf16[256,128]{1,0:T(8,128)(2,1)} %c_ref.1, f32[256,8]{1,0:T(8,128)} %copy.10.log_ref, ...), custom_call_target="tpu_custom_call" | custom-call | tf_op jit(solution)/shard_map/pallas_call | solution.py:488
  92.2 0.0 copy-start
  92.3 1.7 %copy.15 = bf16[256,512]{1,0:T(8,128)(2,1)} copy(bf16[256,512]{1,0:T(8,128)(2,1)} %get-tuple-element.8) | data formatting | bytes 524288
  94.0 0.0 copy-done
  94.0 0.0 copy-start.2
  94.0 0.8 copy.16
  94.8 0.2 copy-done.2
  95.0 0.0 copy-start.1
  95.0 0.7 copy.17
  95.7 0.3 copy-done.1
  96.0 0.7 copy.18
Async XLA Ops:
  92.2 1.7 %copy-start = (bf16[256,1024]{1,0:T(8,128)(2,1)S(1)}, bf16[256,1024]{1,0:T(8,128)(2,1)}, u32[]{:S(2)}) copy-start(bf16[256,1024]{1,0:T(8,128)(2,1)} %get-tuple-element.9) | copy-start | bytes 1572868
  94.0 1.0 %copy-start.2 = (f32[256,128]{1,0:T(8,128)S(1)}, f32[256,128]{1,0:T(8,128)}, u32[]{:S(2)}) copy-start(f32[256,128]{1,0:T(8,128)} %get-tuple-element.10) | copy-start | bytes 393220
  95.0 1.0 copy-start.1

commit v2 on v1

--- a/solution.py
+++ b/solution.py
@@ -40,7 +40,7 @@
     g_s, g_r, st_s, st_r, act_all,
     co_s, co_r, keep, x_s, x_r, y_s, y_r,
     p_s, p_r, px, pf, pf_r, part_ref,
-    y_ss, y_rs, w_ss, w_rs, z_ss, z_rs, c_ss, c_rs, x_ss, x_rs,
+    y_ss, y_rs, w_ss, w_rs, z_ss, z_rs, c_ss, c_rs, x_ss, x_rs, a_ss, a_rs, known,
 ):
     seq, head = lax.axis_index("seq"), lax.axis_index("head")
     z, y = seq // Y, lax.rem(seq, Y)
@@ -67,26 +67,19 @@
     partners = (
         [at_y(d) for d in range(1, Y)]
         + [at_x(d) for d in range(1, X)]
-        + [other]
+        + [other, at_z(1), at_z(-1)]
     )
     for device in partners:
         pl.semaphore_signal(barrier, inc=1, device_id=device, device_id_type=MESH)
 
-    def greet(d, carry):
-        pl.semaphore_signal(barrier, inc=1, device_id=at_z(d), device_id_type=MESH)
-        return carry
-
-    lax.fori_loop(1, Z, greet, 0)
-
     rows = lax.broadcasted_iota(jnp.int32, (T, T), 0)
     lanes = lax.broadcasted_iota(jnp.int32, (T, T), 1)
-    lower = jnp.where(rows >= lanes, 1.0, 0.0).astype(F32)
-    logs = jnp.concatenate([log_ref[...], jnp.zeros((T, K - H), F32)], axis=1)
-    cs = lax.dot_general(
-        lower, logs, NN, precision=lax.Precision.HIGHEST, preferred_element_type=F32
+    upper = jnp.where(rows <= lanes, 1.0, 0.0).astype(F32)
+    cs_rows = lax.dot_general(
+        log_ref[...], upper, NN, precision=lax.Precision.HIGHEST, preferred_element_type=F32
     )
+    cs = jnp.concatenate([cs_rows, jnp.zeros((K - H, T), F32)], axis=0).T
     cs_ref[...] = cs
-    cs_rows = cs.T[0:H]
     csall[y] = cs_rows
     ball[y] = b_ref[...]
     wz[z] = w_ref[...]
@@ -99,38 +92,47 @@
     for i, (left, right) in enumerate(((b_ref, xs_ref), (c_ref, dys_ref))):
         total = dot(left[...], right[...], TN).astype(BF16)
         for h in range(H):
-            up_s[h // 2, i, (h % 2) * K : (h % 2 + 1) * K] = total[:, h * K : (h + 1) * K]
-    up_r[y] = up_s[y]
-
-    pl.semaphore_wait(barrier, Y - 1 + X - 1 + 1 + Z - 1)
+            up_s[i, h // 2, (h % 2) * K : (h % 2 + 1) * K] = total[:, h * K : (h + 1) * K]
+    for i in range(2):
+        up_r[i, y] = up_s[i, y]
+
+    pl.semaphore_wait(barrier, len(partners))
+
+    def tell(k):
+        for d in (1 << k, -(1 << k)):
+            pl.semaphore_signal(known.at[k], inc=1, device_id=at_z(d), device_id_type=MESH)
+
+    def told(k):
+        pl.semaphore_wait(known.at[k], 2)
+
+    rounds = (Z // 2 - 1).bit_length()
+    tell(0)
 
     half = Z // 2
 
-    def w_copies(k):
-        a, b = lax.rem(z - k + Z, Z), lax.rem(z + k, Z)
-        if k < half - 1:
-            fore, back = wz.at[a], wz.at[b]
-        else:
-            fore, back = wz.at[a, 0 : ROWS // 2], wz.at[b, ROWS // 2 : ROWS]
-        return (
-            remote(fore, fore, w_ss.at[0, k], w_rs.at[0, k], at_z(1)),
-            remote(back, back, w_ss.at[1, k], w_rs.at[1, k], at_z(-1)),
+    steps = [(part, side) for part in range(2) for side in range(2)]
+
+    def w_copy(k, part, side, block):
+        here = wz.at[block, part * (ROWS // 2) : (part + 1) * (ROWS // 2)]
+        return remote(
+            here, here, w_ss.at[side, k, part], w_rs.at[side, k, part], at_z(1 - 2 * side)
         )
 
-    def w_arrived(k):
-        a, b = lax.rem(z - 1 - k + Z, Z), lax.rem(z + 1 + k, Z)
-        if k < half - 1:
-            fore, back = wz.at[a], wz.at[b]
-        else:
-            fore, back = wz.at[a, 0 : ROWS // 2], wz.at[b, ROWS // 2 : ROWS]
-        remote(fore, fore, w_ss.at[0, k], w_rs.at[0, k], at_z(1)).wait_recv()
-        remote(back, back, w_ss.at[1, k], w_rs.at[1, k], at_z(-1)).wait_recv()
+    def w_sent(k, part, side):
+        return w_copy(k, part, side, lax.rem(z + (2 * side - 1) * k + Z, Z))
+
+    def w_arrived(k, part, side):
+        w_copy(k, part, side, lax.rem(z + (2 * side - 1) * (k + 1) + Z, Z)).wait_recv()
+
+    def w_steps(k):
+        return [step for step in steps if k < half - 1 or step[0] == step[1]]
 
     def w_step(k):
-        if k > 0:
-            w_arrived(k - 1)
-        for copy in w_copies(k):
-            copy.start()
+        for step in steps:
+            if k > 0:
+                w_arrived(k - 1, *step)
+            if step in w_steps(k):
+                w_sent(k, *step).start()
 
     started = []
 
@@ -148,9 +150,14 @@
                 src_of(y_of(d)), dst_of(y_of(-d)), y_ss.at[group, d], y_rs.at[group, d], at_y(d)
             ).wait_recv()
 
-    y_send(0, lambda t: csall.at[y], lambda s: csall.at[s])
-    y_send(1, lambda t: up_s.at[t], lambda s: up_r.at[s])
-    y_send(2, lambda t: ball.at[y], lambda s: ball.at[s])
+    def cs_of(t):
+        return csall.at[y]
+
+    def up_of(i):
+        return lambda t: up_s.at[i, t], lambda s: up_r.at[i, s]
+
+    y_send(0, cs_of, lambda s: csall.at[s])
+    y_send(1, *up_of(1))
     w_step(0)
 
     below = lanes >= rows
@@ -167,20 +174,26 @@
             wt_ref[...] = weighted if h == 0 else wt_ref[...] + weighted
             own = dot((decay * scores).astype(BF16), dyh)
             actl_ref[:, cut] = own
-            actl_all[y, :, cut] = own.astype(BF16)
-
-    heads(0, 4)
-    y_wait(0, lambda t: csall.at[y], lambda s: csall.at[s])
-    for t in range(Y):
-        atot[t] = jnp.broadcast_to(csall[t][:, T - 1 : T], (H, K))
+            actl_all[y, h // 4, :, (h % 4) * K : (h % 4 + 1) * K] = own.astype(BF16)
+
+    def act_copy(part, side):
+        block = actl_all.at[y, part]
+        return remote(block, block, a_ss.at[part, side], a_rs.at[part, side], at_y(1 - 2 * side))
+
+    def act_arrived(part, side):
+        block = actl_all.at[y_of(2 * side - 1), part]
+        remote(block, block, a_ss.at[part, side], a_rs.at[part, side], at_y(1 - 2 * side)).wait_recv()
+
+    def act_relay(part):
+        block = actl_all.at[y_of(2 * part - 1), part]
+        return remote(block, block, a_ss.at[2, part], a_rs.at[2, part], at_y(1 - 2 * part))
+
+    def act_relayed(part):
+        block = actl_all.at[y_of(2), part]
+        remote(block, block, a_ss.at[2, part], a_rs.at[2, part], at_y(1 - 2 * part)).wait_recv()
 
     def total_of(t, i):
         return atot[t, pl.ds(2 * y + i, 1), :]
-
-    for i in range(2):
-        plane = total_of(0, i) + total_of(1, i) + total_of(2, i) + total_of(3, i)
-        dz_s[4 * i : 4 * i + 4] = jnp.broadcast_to(plane, (4, K))
-    dz_r[z] = dz_s[...]
 
     def z_send(group, src_of, dst):
         def one(d, carry):
@@ -212,25 +225,82 @@
 
         lax.fori_loop(1, Z, one, 0)
 
-    z_send(0, lambda t: dz_s, dz_r)
+    def dz_of(t):
+        return dz_s.at[t // (Z // 2)]
+
+    def z_up(i):
+        return 1 + i, lambda t: zs.at[i, t], zr.at[i]
+
+    def z_down(i):
+        return 3 + i, lambda t: cz.at[i, t], zin.at[i]
+
+    def plane_totals(i):
+        for n in range(2):
+            cut = slice(n * K, (n + 1) * K)
+            spans = range(Y) if i == 0 else range(Y - 1, -1, -1)
+            total = None
+            for t in spans:
+                own = up_r[i, t, cut].astype(F32)
+                total = own if total is None else jnp.exp(total_of(t, n)) * total + own
+            zs[i, n * (Z // 2) : (n + 1) * (Z // 2)] = total.astype(BF16).reshape(
+                Z // 2, 2 * K // Z, K
+            )
+        zr[i, z] = zs[i, z]
+
+    def sweep(i):
+        def one(k, total):
+            j = k if i == 0 else Z - 1 - k
+            cz[i, j] = total.astype(BF16)
+            return jnp.exp(dz_r[j]) * total + zr[i, j].astype(F32)
+
+        lax.fori_loop(0, Z, one, jnp.zeros((2 * K // Z, K), F32))
+        zin[i, z] = cz[i, z]
+
+    def carry_in(i, dst):
+        for n in range(2):
+            cut = slice(n * K, (n + 1) * K)
+            total = zin[i, n * (Z // 2) : (n + 1) * (Z // 2)].reshape(K, K).astype(F32)
+            for t in range(Y) if i == 0 else range(Y - 1, -1, -1):
+                dst[t, cut] = total.astype(BF16)
+                total = jnp.exp(total_of(t, n)) * total + up_r[i, t, cut].astype(F32)
+
+    heads(0, 2)
+    for k in range(1, rounds):
+        told(k - 1)
+        tell(k)
+    heads(2, 4)
     w_step(1)
+    y_wait(0, cs_of, lambda s: csall.at[s])
+    for t in range(Y):
+        atot[t] = jnp.broadcast_to(csall[t][:, T - 1 : T], (H, K))
+    for i in range(2):
+        plane = total_of(0, i) + total_of(1, i) + total_of(2, i) + total_of(3, i)
+        dz_s[i] = plane
+    dz_r[z] = dz_s[z // (Z // 2)]
+    told(rounds - 1)
+    z_send(0, dz_of, dz_r)
+
+    y_wait(1, *up_of(1))
+    plane_totals(1)
+    z_send(*z_up(1))
+    y_send(3, *up_of(0))
+    y_send(2, lambda t: ball.at[y], lambda s: ball.at[s])
+    act_copy(0, 0).start()
+    act_copy(0, 1).start()
+    w_step(2)
     heads(4, 8)
-    w_step(2)
-
-    y_wait(1, lambda t: up_s.at[t], lambda s: up_r.at[s])
-    for i in range(2):
-        cut = slice(i * K, (i + 1) * K)
-        part = slice(i * (Z // 2), (i + 1) * (Z // 2))
-        fore = up_r[0, 0, cut].astype(F32)
-        back = up_r[Y - 1, 1, cut].astype(F32)
-        for t in range(1, Y):
-            fore = jnp.exp(total_of(t, i)) * fore + up_r[t, 0, cut].astype(F32)
-            back = jnp.exp(total_of(Y - 1 - t, i)) * back + up_r[Y - 1 - t, 1, cut].astype(F32)
-        zs[part, 0] = fore.astype(BF16).reshape(Z // 2, 2 * K // Z, K)
-        zs[part, 1] = back.astype(BF16).reshape(Z // 2, 2 * K // Z, K)
-    zr[z] = zs[z]
-    z_send(1, lambda t: zs.at[t], zr)
-    y_send(3, lambda t: actl_all.at[y], lambda s: actl_all.at[s])
+    act_copy(1, 0).start()
+    act_copy(1, 1).start()
+    w_step(3)
+
+    y_wait(3, *up_of(0))
+    plane_totals(0)
+    z_wait(0, dz_of, dz_r)
+    z_wait(*z_up(1))
+    sweep(1)
+    z_send(*z_down(1))
+    z_send(*z_up(0))
+    w_step(4)
 
     y_wait(2, lambda t: ball.at[y], lambda s: ball.at[s])
 
@@ -244,66 +314,52 @@
         return carry
 
     lax.fori_loop(0, Y, tails, 0)
+    act_arrived(0, 0)
+    act_relay(0).start()
+    w_step(5)
+
+    z_wait(*z_down(1))
+    carry_in(1, g_s)
+    g_r[y] = g_s[...]
+    order = (1, 3, 2, 0)
+
+    def grad_copy(k, e):
+        t = y_of(e + order[k])
+        return remote(g_s.at[t], g_r.at[y, t], y_ss.at[4 + k, e], y_rs.at[4 + k, e], at_y(e))
+
+    def grad_wait(k):
+        t = y_of(order[k])
+        for e in (1, 3, 2):
+            remote(
+                g_s.at[t], g_r.at[y_of(-e), t], y_ss.at[4 + k, e], y_rs.at[4 + k, e], at_y(e)
+            ).wait_recv()
+
+    def grad_start(k):
+        for e in (2, 1, 3):
+            grad_copy(k, e).start()
+
+    grad_start(0)
+    grad_start(1)
+    act_arrived(1, 1)
+    act_relay(1).start()
+    grad_start(2)
+    grad_start(3)
+    w_step(6)
+    z_wait(*z_up(0))
+    sweep(0)
+    z_send(*z_down(0))
+    w_step(7)
     wt = wt_ref[...]
     part_ref[0] = dot(wt.astype(BF16), c_ref[...])
     part_ref[1] = dot(wt.T.astype(BF16), b_ref[...])
 
-    z_wait(0, lambda t: dz_s, dz_r)
-    w_step(3)
-    z_wait(1, lambda t: zs.at[t], zr)
-
-    row = 4 * (z // (Z // 2))
-
-    def sweep(k, carry):
-        fore, back = carry
-        j = Z - 1 - k
-        cz[k, 0] = fore.astype(BF16)
-        cz[j, 1] = back.astype(BF16)
-        fore = jnp.exp(dz_r[k, pl.ds(row, 1), :]) * fore + zr[k, 0].astype(F32)
-        back = jnp.exp(dz_r[j, pl.ds(row, 1), :]) * back + zr[j, 1].astype(F32)
-        return fore, back
-
-    zero = jnp.zeros((2 * K // Z, K), F32)
-    lax.fori_loop(0, Z, sweep, (zero, zero))
-    zin[z] = cz[z]
-    z_send(2, lambda t: cz.at[t], zin)
-    w_step(4)
-    w_step(5)
-    z_wait(2, lambda t: cz.at[t], zin)
-
-    for i in range(2):
-        cut = slice(i * K, (i + 1) * K)
-        part = slice(i * (Z // 2), (i + 1) * (Z // 2))
-        back = zin[part, 1].reshape(K, K).astype(F32)
-        for t in reversed(range(Y)):
-            g_s[t, cut] = back.astype(BF16)
-            back = jnp.exp(total_of(t, i)) * back + up_r[t, 1, cut].astype(F32)
-    g_r[y] = g_s[...]
-    y_send(4, lambda t: g_s, lambda s: g_r.at[s])
-    for i in range(2):
-        cut = slice(i * K, (i + 1) * K)
-        part = slice(i * (Z // 2), (i + 1) * (Z // 2))
-        fore = zin[part, 0].reshape(K, K).astype(F32)
-        for t in range(Y):
-            st_s[t, cut] = fore.astype(BF16)
-            fore = jnp.exp(total_of(t, i)) * fore + up_r[t, 0, cut].astype(F32)
-    st_r[y] = st_s[y]
-    y_send(5, lambda t: st_s.at[t], lambda s: st_r.at[s])
-    for k in range(6, half):
-        w_step(k)
-    y_wait(3, lambda t: actl_all.at[y], lambda s: actl_all.at[s])
-    w_arrived(half - 1)
-    y_wait(4, lambda t: g_s, lambda s: g_r.at[s])
-    y_wait(5, lambda t: st_s.at[t], lambda s: st_r.at[s])
-
-    order = (2, 1, 3, 0)
-
     def core_copy(k):
         return remote(co_s.at[k], co_r.at[k], c_ss.at[k], c_rs.at[k], other)
 
     def stage_a(k):
         d = order[k]
         t = y_of(d)
+        grad_wait(k)
         for h in range(H):
             cut = slice(h * K, (h + 1) * K)
             carried = dot(tb_ref[t, h], g_r[h // 2, t, (h % 2) * K : (h % 2 + 1) * K])
@@ -311,8 +367,12 @@
                 own = (actl_ref[:, cut] + carried).astype(BF16)
                 act_ref[:, cut] = own
             else:
-                own = (actl_all[t, :, cut].astype(F32) + carried).astype(BF16)
+                local = actl_all[t, h // 4, :, (h % 4) * K : (h % 4 + 1) * K]
+                own = (local.astype(F32) + carried).astype(BF16)
             act_all[k, :, cut] = own
+        if k == 0:
+            for step in w_steps(half - 1):
+                w_arrived(half - 1, *step)
         act = act_all[k]
         per = Z // X
         for j in range(X):
@@ -342,7 +402,7 @@
 
     def y_copy(k):
         d = order[k]
-        return remote(y_s.at[k], y_r.at[y], y_ss.at[6, d], y_rs.at[6, d], at_y(d))
+        return remote(y_s.at[k], y_r.at[y], y_ss.at[9, d], y_rs.at[9, d], at_y(d))
 
     def stage_c(k):
         total = keep[k, cx]
@@ -386,20 +446,35 @@
         pf[...] = total
         core_total.start()
 
+    def state_of(t):
+        return st_s.at[t]
+
+    def states():
+        z_wait(*z_down(0))
+        carry_in(0, st_s)
+        st_r[y] = st_s[y]
+        y_send(8, state_of, lambda s: st_r.at[s])
+
+    act_arrived(0, 1)
     stage_a(0)
-    parts_start()
+    act_arrived(1, 0)
     stage_a(1)
     stage_b(0)
-    parts_x()
+    states()
+    act_relayed(0)
+    act_relayed(1)
     stage_a(2)
     stage_b(1)
     stage_c(0)
     stage_a(3)
     stage_b(2)
-    parts_core()
+    y_wait(8, state_of, lambda s: st_r.at[s])
+    parts_start()
     stage_c(1)
     stage_b(3)
+    parts_x()
     stage_c(2)
+    parts_core()
     stage_c(3)
     core_total.wait_recv()
     wg_ref[...] = jnp.where(core == 0, pf[...], pf_r[...])
@@ -407,7 +482,7 @@
     for k in range(3):
         d = order[k]
         remote(
-            y_s.at[k], y_r.at[y_of(-d)], y_ss.at[6, d], y_rs.at[6, d], at_y(d)
+            y_s.at[k], y_r.at[y_of(-d)], y_ss.at[9, d], y_rs.at[9, d], at_y(d)
         ).wait_recv()
     for i in range(2):
         pieces = [y_r[t, :, i * ROWS : (i + 1) * ROWS] for t in range(Y)]
@@ -416,11 +491,18 @@
     for copy in started:
         copy.wait_send()
     for k in range(half):
-        for copy in w_copies(k):
-            copy.wait_send()
-    z_sent(0, lambda t: dz_s, dz_r)
-    z_sent(1, lambda t: zs.at[t], zr)
-    z_sent(2, lambda t: cz.at[t], zin)
+        for step in w_steps(k):
+            w_sent(k, *step).wait_send()
+    z_sent(0, dz_of, dz_r)
+    for i in range(2):
+        z_sent(*z_up(i))
+        z_sent(*z_down(i))
+        act_copy(i, 0).wait_send()
+        act_copy(i, 1).wait_send()
+        act_relay(i).wait_send()
+    for k in range(4):
+        for e in range(1, Y):
+            grad_copy(k, e).wait_send()
     for k in range(4):
         core_copy(k).wait_send()
         for copy in x_copies(k):
@@ -447,18 +529,18 @@
             vmem((T, T), F32),
             vmem((Y, H, T), F32),
             vmem((Y, T, K), BF16),
-            vmem((Y, T, H * K), BF16),
+            vmem((Y, 2, T, H * K // 2), BF16),
             vmem((Y, H, T, K), BF16),
             vmem((Y, H, K), F32),
             vmem((Z, ROWS, H * K), BF16),
-            vmem((Y, 2, 2 * K, K), BF16),
-            vmem((Y, 2, 2 * K, K), BF16),
-            vmem((8, K), F32),
-            vmem((Z, 8, K), F32),
-            vmem((Z, 2, piece, K), BF16),
-            vmem((Z, 2, piece, K), BF16),
-            vmem((Z, 2, piece, K), BF16),
-            vmem((Z, 2, piece, K), BF16),
+            vmem((2, Y, 2 * K, K), BF16),
+            vmem((2, Y, 2 * K, K), BF16),
+            vmem((2, 1, K), F32),
+            vmem((Z, 1, K), F32),
+            vmem((2, Z, piece, K), BF16),
+            vmem((2, Z, piece, K), BF16),
+            vmem((2, Z, piece, K), BF16),
+            vmem((2, Z, piece, K), BF16),
             vmem((Y, 2 * K, K), BF16),
             vmem((Y, Y, 2 * K, K), BF16),
             vmem((Y, 2 * K, K), BF16),
@@ -477,11 +559,13 @@
             vmem((T, K), F32),
             vmem((T, K), F32),
             vmem((2, T, K), F32),
-            dma((7, Y)), dma((7, Y)),
-            dma((2, Z // 2)), dma((2, Z // 2)),
-            dma((3, Z)), dma((3, Z)),
+            dma((10, Y)), dma((10, Y)),
+            dma((2, Z // 2, 2)), dma((2, Z // 2, 2)),
+            dma((5, Z)), dma((5, Z)),
             dma((6,)), dma((6,)),
             dma((5, X)), dma((5, X)),
+            dma((3, 2)), dma((3, 2)),
+            pltpu.SemaphoreType.REGULAR(((Z // 2 - 1).bit_length(),)),
         ]
         whole = pl.BlockSpec(memory_space=pltpu.VMEM)
         columns = w_in.shape[0] * mesh.shape["seq"] // mesh.shape["head"]
@@ -499,7 +583,7 @@
             compiler_params=pltpu.CompilerParams(
                 collective_id=0, has_side_effects=True, vmem_limit_bytes=56 * 2**20
             ),
-        )(inner_acts, out_grad, write_proj, read_proj, log_decay, w_in)
+        )(inner_acts, out_grad, write_proj, read_proj, log_decay.T, w_in)
 
     return jax.shard_map(
         local,

time: 96.9 us -> 84.6 us (0.87)
  Pallas kernels: 90.1 us -> 79.4 us
  local copies, waits for them, and re-layouts: 5.84 us -> 4.36 us
    pallas_call x1, Pallas kernels: 90.1 us -> 79.4 us  [local(): pl.pallas_call(functools.partial(kernel, Z, X), out_shape=(jax.ShapeDtype...]
    unnamed x11 -> x10, local copies, waits for them, and re-layouts: 5.84 us -> 4.36 us
where the time goes in v2:
time: 84.6 us; the launch traced here: 84.4 us
  Pallas kernels  79.4 us (94%)
  local copies, waits for them, and re-layouts  4.36 us (5%)
    pallas_call x1, Pallas kernels, local(): pl.pallas_call(functools.partial(kernel, Z, X), out_shape=(jax.ShapeDtype...  79.4 us
    unnamed x10, local copies, waits for them, and re-layouts  4.36 us

profile of v2, /device:TPU:1, one launch (start us, length us, event | category | flops | bytes accessed | tf_op | source)
XLA Modules:
  0.0 84.4 jit_solution(20954224349880664)
XLA Ops:
  0.6 79.4 %shard_map.93 = (bf16[256,512]{1,0:T(8,128)(2,1)}, bf16[256,1024]{1,0:T(8,128)(2,1)}, f32[256,128]{1,0:T(8,128)}, f32[256,128]{1,0:T(8,128)}) custom-call(bf16[256,1024]{1,0:T(8,128)(2,1)} %x_ref.1, bf16[256,1024]{1,0:T(8,128)(2,1)} %dy_ref.1, bf16[256,128]{1,0:T(8,128)(2,1)} %b_ref.1, bf16[256,128]{1,0:T(8,128)(2,1)} %c_ref.1, f32[8,256]{1,0:T(8,128)} %bitcast.1, ...), custom_call_target="tpu_custom_call" | custom-call | tf_op jit(solution)/shard_map/pallas_call | solution.py:572
  80.0 0.0 copy-start
  80.1 1.7 %copy.14 = bf16[256,512]{1,0:T(8,128)(2,1)} copy(bf16[256,512]{1,0:T(8,128)(2,1)} %get-tuple-element.8) | data formatting | bytes 524288
  81.8 0.0 copy-done
  81.8 0.0 copy-start.2
  81.8 0.8 copy.15
  82.6 0.2 copy-done.2
  82.8 0.0 copy-start.1
  82.8 0.7 copy.16
  83.5 0.3 copy-done.1
  83.8 0.7 copy.17
Async XLA Ops:
  80.0 1.7 %copy-start = (bf16[256,1024]{1,0:T(8,128)(2,1)S(1)}, bf16[256,1024]{1,0:T(8,128)(2,1)}, u32[]{:S(2)}) copy-start(bf16[256,1024]{1,0:T(8,128)(2,1)} %get-tuple-element.9) | copy-start | bytes 1572868
  81.8 1.0 %copy-start.2 = (f32[256,128]{1,0:T(8,128)S(1)}, f32[256,128]{1,0:T(8,128)}, u32[]{:S(2)}) copy-start(f32[256,128]{1,0:T(8,128)} %get-tuple-element.10) | copy-start | bytes 393220
  82.8 1.0 %copy-start.1 = (f32[256,128]{1,0:T(8,128)S(1)}, f32[256,128]{1,0:T(8,128)}, u32[]{:S(2)}) copy-start(f32[256,128]{1,0:T(8,128)} %get-tuple-element.11) | copy-start | bytes 393220

commit v3 on v2

--- a/solution.py
+++ b/solution.py
@@ -32,15 +32,15 @@
 
 def kernel(
     Z, X,
-    x_ref, dy_ref, b_ref, c_ref, log_ref, w_ref,
+    x_in, dy_in, b_ref, c_ref, log_ref, w_in,
     out_ref, act_ref, wg_ref, rg_ref,
-    cs_ref, xs_ref, dys_ref, actl_ref, wt_ref,
+    x_ref, dy_ref, w_ref, cs_ref, xs_ref, dys_ref, actl_ref, wt_ref,
     csall, ball, actl_all, tb_ref, atot,
     wz, up_s, up_r, dz_s, dz_r, zs, zr, cz, zin,
     g_s, g_r, st_s, st_r, act_all,
     co_s, co_r, keep, x_s, x_r, y_s, y_r,
     p_s, p_r, px, pf, pf_r, part_ref,
-    y_ss, y_rs, w_ss, w_rs, z_ss, z_rs, c_ss, c_rs, x_ss, x_rs, a_ss, a_rs, known,
+    y_ss, y_rs, w_ss, w_rs, z_ss, z_rs, c_ss, c_rs, x_ss, x_rs, a_ss, a_rs, known, loaded,
 ):
     seq, head = lax.axis_index("seq"), lax.axis_index("head")
     z, y = seq // Y, lax.rem(seq, Y)
@@ -62,6 +62,13 @@
         return (seq, x_of(d) * 2 + core)
 
     other = (seq, cx * 2 + 1 - core)
+
+    loads = [
+        pltpu.make_async_copy(src, dst, loaded.at[i])
+        for i, (src, dst) in enumerate(((x_in, x_ref), (dy_in, dy_ref), (w_in, w_ref)))
+    ]
+    for copy in loads:
+        copy.start()
 
     barrier = pltpu.get_barrier_semaphore()
     partners = (
@@ -82,9 +89,11 @@
     cs_ref[...] = cs
     csall[y] = cs_rows
     ball[y] = b_ref[...]
-    wz[z] = w_ref[...]
     tail = jnp.exp(cs[T - 1 : T] - cs)
     front = jnp.exp(cs)
+    for copy in loads:
+        copy.wait()
+    wz[z] = w_ref[...]
     for h in range(H):
         cut = slice(h * K, (h + 1) * K)
         xs_ref[:, cut] = (x_ref[:, cut].astype(F32) * tail[:, h : h + 1]).astype(BF16)
@@ -467,26 +476,12 @@
     stage_b(1)
     stage_c(0)
     stage_a(3)
-    stage_b(2)
     y_wait(8, state_of, lambda s: st_r.at[s])
     parts_start()
+    stage_b(2)
+    parts_x()
     stage_c(1)
     stage_b(3)
-    parts_x()
-    stage_c(2)
-    parts_core()
-    stage_c(3)
-    core_total.wait_recv()
-    wg_ref[...] = jnp.where(core == 0, pf[...], pf_r[...])
-    rg_ref[...] = jnp.where(core == 0, pf_r[...], pf[...])
-    for k in range(3):
-        d = order[k]
-        remote(
-            y_s.at[k], y_r.at[y_of(-d)], y_ss.at[9, d], y_rs.at[9, d], at_y(d)
-        ).wait_recv()
-    for i in range(2):
-        pieces = [y_r[t, :, i * ROWS : (i + 1) * ROWS] for t in range(Y)]
-        out_ref[:, 2 * i * K : 2 * (i + 1) * K] = jnp.concatenate(pieces, axis=1)
 
     for copy in started:
         copy.wait_send()
@@ -503,6 +498,22 @@
     for k in range(4):
         for e in range(1, Y):
             grad_copy(k, e).wait_send()
+
+    stage_c(2)
+    parts_core()
+    stage_c(3)
+    core_total.wait_recv()
+    wg_ref[...] = jnp.where(core == 0, pf[...], pf_r[...])
+    rg_ref[...] = jnp.where(core == 0, pf_r[...], pf[...])
+    for k in range(3):
+        d = order[k]
+        remote(
+            y_s.at[k], y_r.at[y_of(-d)], y_ss.at[9, d], y_rs.at[9, d], at_y(d)
+        ).wait_recv()
+    for i in range(2):
+        pieces = [y_r[t, :, i * ROWS : (i + 1) * ROWS] for t in range(Y)]
+        out_ref[:, 2 * i * K : 2 * (i + 1) * K] = jnp.concatenate(pieces, axis=1)
+
     for k in range(4):
         core_copy(k).wait_send()
         for copy in x_copies(k):
@@ -522,6 +533,9 @@
 
     def local(inner_acts, out_grad, write_proj, read_proj, log_decay, w_in):
         scratch = [
+            vmem((T, H * K), BF16),
+            vmem((T, H * K), BF16),
+            vmem((ROWS, H * K), BF16),
             vmem((T, K), F32),
             vmem((T, H * K), BF16),
             vmem((T, H * K), BF16),
@@ -566,8 +580,10 @@
             dma((5, X)), dma((5, X)),
             dma((3, 2)), dma((3, 2)),
             pltpu.SemaphoreType.REGULAR(((Z // 2 - 1).bit_length(),)),
+            dma((3,)),
         ]
         whole = pl.BlockSpec(memory_space=pltpu.VMEM)
+        hbm = pl.BlockSpec(memory_space=pl.ANY)
         columns = w_in.shape[0] * mesh.shape["seq"] // mesh.shape["head"]
         return pl.pallas_call(
             functools.partial(kernel, Z, X),
@@ -577,7 +593,7 @@
                 jax.ShapeDtypeStruct((T, K), F32),
                 jax.ShapeDtypeStruct((T, K), F32),
             ),
-            in_specs=[whole] * 6,
+            in_specs=[hbm, hbm, whole, whole, whole, hbm],
             out_specs=(whole,) * 4,
             scratch_shapes=scratch,
             compiler_params=pltpu.CompilerParams(

time: 84.6 us -> 82.4 us (0.974)
  Pallas kernels: 79.4 us -> 77.2 us
    pallas_call x1, Pallas kernels: 79.4 us -> 77.2 us  [local(): pl.pallas_call(functools.partial(kernel, Z, X), out_shape=(jax.ShapeDtype...]
where the time goes in v3:
time: 82.4 us; the launch traced here: 82.2 us
  Pallas kernels  77.2 us (94%)
  local copies, waits for them, and re-layouts  4.36 us (5%)
    pallas_call x1, Pallas kernels, local(): pl.pallas_call(functools.partial(kernel, Z, X), out_shape=(jax.ShapeDtype...  77.2 us
    unnamed x10, local copies, waits for them, and re-layouts  4.36 us

profile of v3, /device:TPU:1, one launch (start us, length us, event | category | flops | bytes accessed | tf_op | source)
XLA Modules:
  0.0 82.2 jit_solution(14857174095411416133)
XLA Ops:
  0.6 77.2 %shard_map.93 = (bf16[256,512]{1,0:T(8,128)(2,1)}, bf16[256,1024]{1,0:T(8,128)(2,1)}, f32[256,128]{1,0:T(8,128)}, f32[256,128]{1,0:T(8,128)}) custom-call(bf16[256,1024]{1,0:T(8,128)(2,1)} %x_in.1, bf16[256,1024]{1,0:T(8,128)(2,1)} %dy_in.1, bf16[256,128]{1,0:T(8,128)(2,1)} %b_ref.1, bf16[256,128]{1,0:T(8,128)(2,1)} %c_ref.1, f32[8,256]{1,0:T(8,128)} %bitcast.1, ...), custom_call_target="tpu_custom_call" | custom-call | tf_op jit(solution)/shard_map/pallas_call | solution.py:588
  77.8 0.0 copy-start
  77.8 1.7 %copy.14 = bf16[256,512]{1,0:T(8,128)(2,1)} copy(bf16[256,512]{1,0:T(8,128)(2,1)} %get-tuple-element.8) | data formatting | bytes 524288
  79.5 0.0 copy-done
  79.5 0.0 copy-start.2
  79.5 0.8 copy.15
  80.3 0.2 copy-done.2
  80.6 0.0 copy-start.1
  80.6 0.7 copy.16
  81.2 0.3 copy-done.1
  81.5 0.7 copy.17
Async XLA Ops:
  77.8 1.7 %copy-start = (bf16[256,1024]{1,0:T(8,128)(2,1)S(1)}, bf16[256,1024]{1,0:T(8,128)(2,1)}, u32[]{:S(2)}) copy-start(bf16[256,1024]{1,0:T(8,128)(2,1)} %get-tuple-element.9) | copy-start | bytes 1572868
  79.5 1.0 %copy-start.2 = (f32[256,128]{1,0:T(8,128)S(1)}, f32[256,128]{1,0:T(8,128)}, u32[]{:S(2)}) copy-start(f32[256,128]{1,0:T(8,128)} %get-tuple-element.10) | copy-start | bytes 393220
  80.6 1.0 %copy-start.1 = (f32[256,128]{1,0:T(8,128)S(1)}, f32[256,128]{1,0:T(8,128)}, u32[]{:S(2)}) copy-start(f32[256,128]{1,0:T(8,128)} %get-tuple-element.11) | copy-start | bytes 393220
